TPU v7x, 32 devices: a whole 2x2x4 slice. The times are simulated.
32 devices in a mesh: groups: 2 (over y), expert: 4 (over z), helper: 4 (over x, core).
Axes of the slice: x: 2, y: 2, z: 4, core: 2. Of those that a mesh axis runs over, the one named last changes fastest.
Arguments:
- tokens: bfloat16 [256, 3584], P(('groups', 'expert'), 'helper'), parts along dimension 0, may hold values from -6 to 6
- up_weight: bfloat16 [64, 3584, 1024], P('expert', None, 'helper'), may hold values from -0.09375 to 0.09375
- down_weight: bfloat16 [64, 1024, 3584], P('expert', 'helper'), may hold values from -0.1875 to 0.1875
- expert_ids: int32 [256, 8], P(('groups', 'expert')), parts along dimension 0, may hold values from 0 to 63, all different within a row; in each aligned block of 32 rows (0 to 31, 32 to 63, ...) at most 8 rows name the same one
- route_scores: float32 [256, 8], P(('groups', 'expert')), parts along dimension 0, may hold values from 0.1 to 1
Outputs:
- layer_out: bfloat16 [256, 3584], P(('groups', 'expert'), 'helper'), parts along dimension 0
There are 2 independent parts, one for each index of `groups`. A program takes and returns all parts, laid end to end along the dimension named above; an argument that names none is the same for every part. Nothing has to cross between parts.
Inputs may be any that keep to these rules, and one draw needn't show every extreme that they name: `expert_ids`: each token names 8 different experts. In each aligned block of 32 tokens (the tokens of one index of expert) no expert is named by more than 8 tokens, a bound that some block reaches.
All inputs are finite; a program needn't handle non-finite values.
Results may differ from a plain program's by a relative error of at most 0.012.
Values may be sent and summed in bfloat16 or wider, within the bound.
A program may use at most 192 MiB of HBM per device.

v0:
```python
import jax
import jax.numpy as jnp
from jax import lax
from jax.sharding import PartitionSpec as P

CAP = 8


def into_experts(received, expert_ranks, local_count):
    columns_in = received.shape[2]
    shaped = received.reshape(expert_ranks, local_count, CAP, columns_in)
    return shaped.transpose(1, 0, 2, 3).reshape(local_count, expert_ranks * CAP, columns_in)


def into_sources(results, expert_ranks, local_count):
    columns_in = results.shape[2]
    shaped = results.reshape(local_count, expert_ranks, CAP, columns_in)
    return shaped.transpose(1, 0, 2, 3).reshape(expert_ranks, local_count * CAP, columns_in)


def local(tokens, up_weight, down_weight, expert_ids, route_scores):
    expert_ranks = lax.axis_size("expert")
    local_count = up_weight.shape[0]
    all_experts = local_count * expert_ranks
    slot_count = all_experts * CAP
    gate_weight = 2.5 * route_scores / jnp.sum(route_scores, axis=1, keepdims=True)
    expert_iota = jnp.arange(all_experts, dtype=jnp.int32)
    chosen = jnp.sum(
        (expert_ids[:, :, None] == expert_iota[None, None, :]).astype(jnp.int32), axis=1
    )
    before = jnp.cumsum(chosen, axis=0) - chosen
    position = jnp.take_along_axis(before, expert_ids, axis=1)
    slot_index = expert_ids * CAP + position
    slot_iota = jnp.arange(slot_count, dtype=jnp.int32)
    placing = jnp.sum(
        (slot_iota[:, None, None] == slot_index[None, :, :]).astype(jnp.bfloat16), axis=2
    )
    match_table = slot_index[:, :, None] == slot_iota[None, None, :]
    weighting = jnp.sum(jnp.where(match_table, gate_weight[:, :, None], 0.0), axis=1)
    full_tokens = lax.all_gather(tokens, "helper", axis=1, tiled=True)
    outgoing = jnp.dot(placing, full_tokens, preferred_element_type=jnp.float32).astype(
        jnp.bfloat16
    )
    outgoing = outgoing.reshape(expert_ranks, local_count * CAP, full_tokens.shape[1])
    received = lax.all_to_all(outgoing, "expert", split_axis=0, concat_axis=0, tiled=True)
    expert_rows = into_experts(received, expert_ranks, local_count)
    projected = jnp.einsum(
        "erd,edf->erf", expert_rows, up_weight, preferred_element_type=jnp.float32
    )
    hidden = jax.nn.silu(projected).astype(jnp.bfloat16)
    partial_value = jnp.einsum(
        "erf,efd->erd", hidden, down_weight, preferred_element_type=jnp.float32
    ).astype(jnp.bfloat16)
    summed = (
        lax.psum_scatter(partial_value, "helper", scatter_dimension=2, tiled=True)
        .astype(jnp.float32)
        .astype(jnp.bfloat16)
    )
    returning = into_sources(summed, expert_ranks, local_count)
    arrived = lax.all_to_all(returning, "expert", split_axis=0, concat_axis=0, tiled=True)
    slot_results = arrived.reshape(slot_count, arrived.shape[2])
    layer_out = jnp.dot(
        weighting, slot_results.astype(jnp.float32), precision=lax.Precision.HIGHEST
    )
    return layer_out.astype(jnp.bfloat16)


def solution(mesh):
    return jax.shard_map(
        local,
        mesh=mesh,
        in_specs=(
            P(("groups", "expert"), "helper"),
            P("expert", None, "helper"),
            P("expert", "helper", None),
            P(("groups", "expert"), None),
            P(("groups", "expert"), None),
        ),
        out_specs=P(("groups", "expert"), "helper"),
        check_vma=False,
    )
```

profile of v0, /device:TPU:0, one launch (start us, length us, event | category | flops | bytes accessed | tf_op | source)
XLA Modules:
  0.0 256.1 jit_solution(9854045012022172827)
XLA Ops:
  6.5 0.0 reduce-scatter.4.cloned.1.call-start
  6.5 0.8 copy.34
  7.3 0.1 convert_reduce_fusion
  7.4 0.1 reduce_window_sum.11
  7.5 0.1 reshape.39
  7.6 0.0 copy-start
  7.6 1.9 gather_fusion
  9.6 0.1 reshape.42
  9.7 0.2 fusion.8
  9.9 0.0 copy-done
  9.9 7.0 %all_gather.3 = bf16[32,3584]{1,0:T(8,128)(2,1)S(1)} all-gather(bf16[32,896]{1,0:T(8,128)(2,1)S(1)} %copy-done), channel_id=1, replica_groups=mesh['groups'=2,'expert'=4,'helper'=4] {'helper'}, dimensions={1}, use_global_device_ids=true | all-gather | bytes 286720 | tf_op jit(solution)/shard_map/all_gather | solution.py:40
  16.9 1.1 convolution_convert_fusion.1
  18.1 87.3 %all_to_all.10 = bf16[4,128,3584]{2,1,0:T(8,128)(2,1)} all-to-all(bf16[4,128,3584]{2,1,0:T(8,128)(2,1)S(1)} %bitcast.36), channel_id=1, replica_groups=mesh['groups'=2,'expert'=4,'helper'=4] {'expert'}, dimensions={0} | all-to-all | bytes 7340032 | tf_op jit(solution)/shard_map/all_to_all | solution.py:45
  105.4 28.0 %convolution_convert_fusion = bf16[16,32,3584]{2,1,0:T(8,128)(2,1)} fusion(bf16[16,256,3584]{2,1,0:T(8,128)(2,1)} %param.7, bf16[16,3584,256]{2,1,0:T(8,128)(2,1)} %param.6, bf16[4,128,3584]{2,1,0:T(8,128)(2,1)} %all_to_all.10), kind=kOutput, calls=%fused_computation.1 | convolution fusion | flops 1881538560 | bytes 66060288 | tf_op jit(solution)/shard_map/erf,efd->erd/dot_general | solution.py:51
  133.4 16.1 %copy.42 = bf16[16,32,3584]{1,0,2:T(8,128)(2,1)} copy(bf16[16,32,3584]{2,1,0:T(8,128)(2,1)} %convolution_convert_fusion) | data formatting | bytes 7340032
  149.5 19.9 %reshape.50 = bf16[3584,512]{1,0:T(8,128)(2,1)} reshape(bf16[3584,16,32]{2,1,0:T(8,128)(2,1)} %bitcast.35) | data formatting | bytes 7340032
  169.4 0.0 reduce-scatter.4.cloned.1.call-update
  169.4 40.5 %reduce-scatter.4.cloned.1.call-done = bf16[896,512]{1,0:T(8,128)(2,1)} async-done(((bf16[3584,512]{1,0:T(8,128)(2,1)}), bf16[896,512]{1,0:T(8,128)(2,1)}) %reduce-scatter.4.cloned.1.call-update) | async-done | bytes 917520
  209.9 5.1 %reshape.51 = bf16[896,16,32]{2,1,0:T(8,128)(2,1)} reshape(bf16[896,512]{1,0:T(8,128)(2,1)} %reduce-scatter.4.cloned.1.call-done) | data formatting | bytes 1835008
  215.1 0.0 copy-start.1
  215.1 4.5 %copy.43 = bf16[16,32,896]{2,1,0:T(8,128)(2,1)S(1)} copy(bf16[16,32,896]{1,0,2:T(8,128)(2,1)} %bitcast.37) | data formatting | bytes 1835008
  219.6 1.0 copy_bitcast_fusion
  220.6 4.6 %all-to-all-start.1 = ((bf16[4,128,896]{2,1,0:T(8,128)(2,1)}), bf16[4,128,896]{2,1,0:T(8,128)(2,1)S(1)}, u32[]{:S(2)}, u32[]{:S(2)}) async-start(bf16[4,128,896]{2,1,0:T(8,128)(2,1)} %copy_bitcast_fusion), calls=%async_computation.1 | async-start | bytes 1835008 | tf_op jit(solution)/shard_map/all_to_all | solution.py:60
  225.2 0.0 copy-done.1
  225.2 0.1 copy.39
  225.3 0.2 select_reduce_fusion
  225.5 22.6 %all-to-all-done.1 = bf16[4,128,896]{2,1,0:T(8,128)(2,1)S(1)} async-done(((bf16[4,128,896]{2,1,0:T(8,128)(2,1)}), bf16[4,128,896]{2,1,0:T(8,128)(2,1)S(1)}, u32[]{:S(2)}, u32[]{:S(2)}) %all-to-all-start.1) | async-done | bytes 917536 | tf_op jit(solution)/shard_map/all_to_all | solution.py:60
  248.1 1.2 convolution_convert_fusion.2
  (5 shorter events, 0.1 us)
Async XLA Ops:
  6.5 203.4 %reduce-scatter.4.cloned.1.call-start = ((), (), s32[]{:S(2)}) async-start(), calls=%async_computation.3 | async-start | bytes 4587520
  7.6 2.3 copy-start
  215.1 10.1 %copy-start.1 = (f32[32,8]{0,1:T(8,128)S(1)}, f32[32,8]{0,1:T(8,128)}, u32[]{:S(2)}) copy-start(f32[32,8]{0,1:T(8,128)} %param.9) | copy-start | bytes 3076
  220.6 27.5 %all-to-all-start.1 = ((bf16[4,128,896]{2,1,0:T(8,128)(2,1)}), bf16[4,128,896]{2,1,0:T(8,128)(2,1)S(1)}, u32[]{:S(2)}, u32[]{:S(2)}) async-start(bf16[4,128,896]{2,1,0:T(8,128)(2,1)} %copy_bitcast_fusion), calls=%async_computation.1 | async-start | bytes 1835008 | tf_op jit(solution)/shard_map/all_to_all | solution.py:60
Sparse Core Ops, SparseCore 0:
  169.5 40.3 reduce-scatter.3
where the time goes:
time: 257 us; the launch traced here: 256 us
  blocking collectives  94.3 us (37%)
  waiting for transfers between devices  63.1 us (25%)
  local copies, waits for them, and re-layouts  49.6 us (19%)
  matrix products  30.3 us (12%)
  between operations  13.5 us (5%)
  starting transfers between devices  4.61 us (2%)
    all_to_all x1, blocking collectives, local(): lax.all_to_all(outgoing, 'expert', split_axis=0, concat_axis=0, tiled=True)  87.3 us
    unnamed x9, local copies, waits for them, and re-layouts  46.4 us
    unnamed x2, waiting for transfers between devices  40.5 us
    dot_general x1, matrix products, local(): jnp.einsum('erf,efd->erd', hidden, down_weight, preferred_element_type=jn...  28 us
    all_to_all x1, waiting for transfers between devices, local(): lax.all_to_all(returning, 'expert', split_axis=0, concat_axis=0, tiled=True)  22.6 us
    all_gather x1, blocking collectives, local(): full_tokens = lax.all_gather(tokens, 'helper', axis=1, tiled=True)  7.02 us
  transfers between devices with their start and end apart: 2, of which 2 were waited for; matrix products, arithmetic and copies ran while one was open for 0% of the time, Pallas kernels for 0%

commit v1 on v0

v1 whole, which is shorter than its diff:
```python
import jax
import jax.numpy as jnp
from jax import lax
from jax.sharding import PartitionSpec as P


def local(tokens, up_weight, down_weight, expert_ids, route_scores):
    expert_ranks = lax.axis_size("expert")
    local_count = up_weight.shape[0]
    all_experts = local_count * expert_ranks
    gate_weight = 2.5 * route_scores / jnp.sum(route_scores, axis=1, keepdims=True)
    expert_iota = jnp.arange(all_experts, dtype=jnp.int32)
    table = jnp.sum(
        jnp.where(expert_ids[:, :, None] == expert_iota, gate_weight[:, :, None], 0.0), axis=1
    )
    full = lax.all_gather(tokens, "expert", axis=0, tiled=True)
    full = lax.all_gather(full, "helper", axis=1, tiled=True)
    share = lax.all_to_all(
        table.reshape(-1, expert_ranks, local_count).transpose(1, 0, 2),
        "expert", split_axis=0, concat_axis=0, tiled=True,
    ).reshape(-1, local_count)
    projected = jnp.einsum("td,edf->etf", full, up_weight, preferred_element_type=jnp.float32)
    hidden = (jax.nn.silu(projected) * share.T[:, :, None]).astype(jnp.bfloat16)
    total = jnp.einsum("etf,efd->td", hidden, down_weight, preferred_element_type=jnp.float32)
    total = lax.psum_scatter(total.astype(jnp.bfloat16), "helper", scatter_dimension=1, tiled=True)
    return lax.psum_scatter(total, "expert", scatter_dimension=0, tiled=True)


def solution(mesh):
    return jax.shard_map(
        local,
        mesh=mesh,
        in_specs=(
            P(("groups", "expert"), "helper"),
            P("expert", None, "helper"),
            P("expert", "helper", None),
            P(("groups", "expert"), None),
            P(("groups", "expert"), None),
        ),
        out_specs=P(("groups", "expert"), "helper"),
        check_vma=False,
    )
```

time: 257 us -> 122 us (0.47)
  blocking collectives: 94.3 us -> 23.8 us
  local copies, waits for them, and re-layouts: 49.6 us -> 5.34 us
  waiting for transfers between devices: 63.1 us -> 44.6 us
  matrix products: 30.3 us -> 25.4 us
    all_to_all x1 -> x0, blocking collectives: 87.3 us -> none  [local(): lax.all_to_all(outgoing, 'expert', split_axis=0, concat_axis=0, tiled=True)]
    unnamed x9 -> x5, local copies, waits for them, and re-layouts: 46.4 us -> 4.57 us
    all_to_all x1, waiting for transfers between devices: 22.6 us -> 0.01 us  [local(): lax.all_to_all(table.reshape(-1, expert_ranks, local_count).transpose(1,...]
    reduce_scatter x0 -> x1, waiting for transfers between devices: none -> 20.1 us  [local(): return lax.psum_scatter(total, 'expert', scatter_dimension=0, tiled=True)]
    all_gather x1 -> x2, blocking collectives: 7.02 us -> 23.8 us  [the longest x1 14.5 us: local(): full = lax.all_gather(tokens, 'expert', axis=0, tiled=True)]
    unnamed x2 -> x3, waiting for transfers between devices: 40.5 us -> 24.4 us
    dot_general x3 -> x1, matrix products: 30.3 us -> 25.4 us  [local(): jnp.einsum('etf,efd->td', hidden, down_weight, preferred_element_type=jnp...]
  transfers between devices with their start and end apart: 2 -> 3, of which waited for: 2 -> 2; matrix products, arithmetic and copies ran while one was open for 0% -> 0% of each run, Pallas kernels for 0% -> 0%
where the time goes in v1:
time: 122 us; the launch traced here: 121 us
  waiting for transfers between devices  44.6 us (37%)
  matrix products  25.4 us (21%)
  blocking collectives  23.8 us (20%)
  between operations  13.4 us (11%)
  starting transfers between devices  6.36 us (5%)
  local copies, waits for them, and re-layouts  5.34 us (4%)
  other arithmetic  2.21 us (2%)
    dot_general x1, matrix products, local(): jnp.einsum('etf,efd->td', hidden, down_weight, preferred_element_type=jnp...  25.4 us
    unnamed x3, waiting for transfers between devices  24.4 us
    reduce_scatter x1, waiting for transfers between devices, local(): return lax.psum_scatter(total, 'expert', scatter_dimension=0, tiled=True)  20.1 us
    all_gather x1, blocking collectives, local(): full = lax.all_gather(tokens, 'expert', axis=0, tiled=True)  14.5 us
    all_gather x1, blocking collectives, local(): full = lax.all_gather(full, 'helper', axis=1, tiled=True)  9.3 us
    all_to_all x1, starting transfers between devices, local(): lax.all_to_all(table.reshape(-1, expert_ranks, local_count).transpose(1,...  6.32 us
    unnamed x5, local copies, waits for them, and re-layouts  4.57 us
  transfers between devices with their start and end apart: 3, of which 2 were waited for; matrix products, arithmetic and copies ran while one was open for 0% of the time, Pallas kernels for 0%

profile of v1, /device:TPU:0, one launch (start us, length us, event | category | flops | bytes accessed | tf_op | source)
XLA Modules:
  0.0 121.2 jit_solution(1434396289398457247)
XLA Ops:
  6.5 0.7 reduce_sum.18
  7.2 0.7 multiply_divide_fusion
  7.9 0.1 copy.26
  8.0 0.8 copy.25
  8.8 0.1 select_reduce_fusion
  8.9 0.1 copy.27
  9.0 0.7 reshape.16
  9.7 6.3 %all-to-all-start = ((f32[4,1,512]{2,1,0:T(1,128)}), f32[4,1,512]{2,1,0:T(1,128)S(1)}, u32[]{:S(2)}, u32[]{:S(2)}) async-start(f32[4,1,512]{2,1,0:T(1,128)} %reshape.16), calls=%async_computation | async-start | bytes 16384 | tf_op jit(solution)/shard_map/all_to_all | solution.py:18
  16.0 0.0 reduce-scatter.7.cloned.1.call-start
  16.0 14.5 %all_gather.6 = bf16[128,896]{1,0:T(8,128)(2,1)S(1)} all-gather(bf16[32,896]{1,0:T(8,128)(2,1)} %param.5), channel_id=1, replica_groups=mesh['groups'=2,'expert'=4,'helper'=4] {'expert'}, dimensions={0}, use_global_device_ids=true | all-gather | bytes 286720 | tf_op jit(solution)/shard_map/all_gather | solution.py:16
  30.6 9.3 %all_gather.7 = bf16[128,3584]{1,0:T(8,128)(2,1)S(1)} all-gather(bf16[128,896]{1,0:T(8,128)(2,1)S(1)} %all_gather.6), channel_id=1, replica_groups=mesh['groups'=2,'expert'=4,'helper'=4] {'helper'}, dimensions={1}, use_global_device_ids=true | all-gather | bytes 1146880 | tf_op jit(solution)/shard_map/all_gather | solution.py:17
  39.9 0.0 all-to-all-done
  39.9 0.5 broadcast.6
  40.4 0.7 reduce
  41.0 0.1 reshape.17
  41.2 0.1 reshape.11
  41.2 25.4 %fusion = bf16[128,3584]{1,0:T(8,128)(2,1)S(1)} fusion(bf16[16,256,3584]{2,1,0:T(8,128)(2,1)} %param.7, bf16[16,3584,256]{2,1,0:T(8,128)(2,1)} %param.6, f32[16,128]{1,0:T(8,128)S(1)} %bitcast.41, bf16[128,3584]{1,0:T(8,128)(2,1)S(1)} %all_gather.7), kind=kOutput, calls=%fused_computation.1 | convolution fusion | flops 7519797248 | bytes 60563456 | tf_op jit(solution)/shard_map/etf,efd->td/dot_general | solution.py:24
  66.7 1.3 %copy.32 = bf16[128,3584]{0,1:T(8,128)(2,1)} copy(bf16[128,3584]{1,0:T(8,128)(2,1)S(1)} %fusion) | data formatting | bytes 1835008
  68.0 0.0 reduce-scatter.7.cloned.1.call-update
  68.0 0.0 reduce-scatter.5.cloned.1.call-start
  68.1 24.4 %reduce-scatter.7.cloned.1.call-done = bf16[896,128]{1,0:T(8,128)(2,1)} async-done(((bf16[3584,128]{1,0:T(8,128)(2,1)}), bf16[896,128]{1,0:T(8,128)(2,1)}) %reduce-scatter.7.cloned.1.call-update) | async-done | bytes 229392
  92.4 1.7 %copy.33 = bf16[128,896]{1,0:T(8,128)(2,1)} copy(bf16[128,896]{0,1:T(8,128)(2,1)} %bitcast.38) | data formatting | bytes 458752
  94.2 0.0 reduce-scatter.5.cloned.1.call-update
  94.2 20.1 %reduce-scatter.5.cloned.1.call-done = bf16[32,896]{1,0:T(8,128)(2,1)} async-done(((bf16[128,896]{1,0:T(8,128)(2,1)}), bf16[32,896]{1,0:T(8,128)(2,1)}) %reduce-scatter.5.cloned.1.call-update) | async-done | bytes 57360 | tf_op jit(solution)/shard_map/reduce_scatter | solution.py:26
  (1 shorter events, 0.0 us)
Async XLA Ops:
  9.7 30.2 %all-to-all-start = ((f32[4,1,512]{2,1,0:T(1,128)}), f32[4,1,512]{2,1,0:T(1,128)S(1)}, u32[]{:S(2)}, u32[]{:S(2)}) async-start(f32[4,1,512]{2,1,0:T(1,128)} %reshape.16), calls=%async_computation | async-start | bytes 16384 | tf_op jit(solution)/shard_map/all_to_all | solution.py:18
  16.0 76.4 %reduce-scatter.7.cloned.1.call-start = ((), (), s32[]{:S(2)}) async-start(), calls=%async_computation.4 | async-start | bytes 1146880
  68.0 46.4 %reduce-scatter.5.cloned.1.call-start = ((), (), s32[]{:S(2)}) async-start(), calls=%async_computation.3 | async-start | bytes 286720 | tf_op jit(solution)/shard_map/reduce_scatter | solution.py:26
Sparse Core Ops, SparseCore 0:
  68.1 24.2 reduce-scatter.6
  94.8 19.5 reduce-scatter.4

commit v2 on v1

--- a/solution.py
+++ b/solution.py
@@ -1,10 +1,18 @@
+import functools
+
 import jax
 import jax.numpy as jnp
 from jax import lax
+from jax.experimental import pallas as pl
+from jax.experimental.pallas import tpu as pltpu
 from jax.sharding import PartitionSpec as P
 
-
-def local(tokens, up_weight, down_weight, expert_ids, route_scores):
+TILE = 256
+LANES = 128
+MESH = pl.DeviceIdType.MESH
+
+
+def spread(tokens, up_weight, down_weight, expert_ids, route_scores):
     expert_ranks = lax.axis_size("expert")
     local_count = up_weight.shape[0]
     all_experts = local_count * expert_ranks
@@ -26,6 +34,286 @@
     return lax.psum_scatter(total, "expert", scatter_dimension=0, tiled=True)
 
 
+def fused_kernel(
+    ranks, tokens, ids, scores, up, down, out,
+    weights, near, far, gates, tables, acc, hidden, sums_far, sums_near,
+    got_far, pass_far, got_x, got_near, pass_z, got_z,
+    weight_sem, z_send, z_recv, g_send, g_recv, c_send, c_recv, x_send, x_recv,
+    f_send, f_recv, p_send, p_recv, r_send, r_recv,
+):
+    rows, width = tokens.shape
+    experts, ktiles = up.shape[0], up.shape[1] // 2
+    chunks = ktiles
+    group = experts * ktiles
+    me = lax.axis_index("expert")
+    helper = lax.axis_index("helper")
+    core, chip = lax.rem(helper, 2), helper // 2
+    core_peer = {"helper": chip * 2 + 1 - core}
+    chip_peer = {"helper": (1 - chip) * 2 + core}
+    columns = pl.ds(pl.multiple_of(core * width, LANES), width)
+    other_columns = pl.ds(pl.multiple_of((1 - core) * width, LANES), width)
+
+    def rank_at(step):
+        return lax.rem(me + step, ranks)
+
+    def rows_of(rank):
+        return pl.ds(pl.multiple_of(rank * rows, rows), rows)
+
+    def load_up(part, e):
+        half = chip if part == 0 else 1 - chip
+        return pltpu.make_async_copy(
+            up.at[e, pl.ds(half * ktiles, ktiles)],
+            weights.at[pl.ds(part * group + e * ktiles, ktiles)],
+            weight_sem.at[part * experts + e],
+        )
+
+    def chunk_at(i):
+        return jnp.where(core == 1, i, chunks - 1 - i)
+
+    def load_down(part, i):
+        half = 1 - chip if part == 0 else chip
+        first = 2 * group if part == 0 else 0
+        column = pl.multiple_of((half * chunks + chunk_at(i)) * TILE, TILE)
+        return pltpu.make_async_copy(
+            down.at[:, :, pl.ds(column, TILE)],
+            weights.at[pl.ds(first + i * experts, experts)],
+            weight_sem.at[2 * experts + part * chunks + i],
+        )
+
+    def remote(src, dst, send, recv, device):
+        return pltpu.make_async_remote_copy(
+            src_ref=src, dst_ref=dst, send_sem=send, recv_sem=recv,
+            device_id=device, device_id_type=MESH,
+        )
+
+    def each(count, body):
+        lax.fori_loop(0, count, lambda i, c: (body(i), c)[1], 0)
+
+    barrier = pltpu.get_barrier_semaphore()
+    for step in range(1, ranks):
+        pl.semaphore_signal(barrier, inc=1, device_id={"expert": rank_at(step)}, device_id_type=MESH)
+    pl.semaphore_signal(barrier, inc=1, device_id=core_peer, device_id_type=MESH)
+    pl.semaphore_signal(barrier, inc=1, device_id=chip_peer, device_id_type=MESH)
+    each(experts, lambda e: load_up(0, e).start())
+    near[rows_of(me), columns] = tokens[...]
+    score = scores[...]
+    gate = 2.5 * score / jnp.sum(score, axis=1, keepdims=True)
+    named = ids[...]
+    lane = lax.broadcasted_iota(jnp.int32, (rows, LANES), 1)
+    for step in range(ranks):
+        base = rank_at(step) * experts
+        total = jnp.zeros((rows, LANES), jnp.float32)
+        for k in range(named.shape[1]):
+            hit = named[:, k:k + 1] - base == lane
+            total = total + jnp.where(hit, gate[:, k:k + 1], 0.0)
+        if step == 0:
+            gates[rows_of(me), :] = total
+        else:
+            tables[step - 1] = total
+    pl.semaphore_wait(barrier, ranks + 1)
+
+    def z_copy(step):
+        here = near.at[rows_of(me), columns]
+        return remote(here, here, z_send.at[step - 1], z_recv.at[step - 1], {"expert": rank_at(step)})
+
+    def z_wait(step):
+        there = near.at[rows_of(rank_at(ranks - step)), columns]
+        remote(there, there, z_send.at[step - 1], z_recv.at[step - 1], {"expert": rank_at(step)}).wait_recv()
+
+    def g_copy(step):
+        return remote(
+            tables.at[step - 1], gates.at[rows_of(me), :],
+            g_send.at[step - 1], g_recv.at[step - 1], {"expert": rank_at(step)},
+        )
+
+    def c_copy(step):
+        place = near.at[rows_of(rank_at(ranks - step)), columns]
+        return remote(place, place, c_send.at[step], c_recv.at[step], core_peer)
+
+    def x_copy(step):
+        place = rows_of(rank_at(ranks - step))
+        return remote(near.at[place, columns], far.at[place, columns], x_send.at[step], x_recv.at[step], chip_peer)
+
+    def f_copy(step):
+        place = far.at[rows_of(rank_at(ranks - step)), columns]
+        return remote(place, place, f_send.at[step], f_recv.at[step], core_peer)
+
+    for step in range(1, ranks):
+        z_copy(step).start()
+    x_copy(0).start()
+    c_copy(0).start()
+    for step in range(1, ranks):
+        g_copy(step).start()
+    each(experts, lambda e: load_up(1, e).start())
+    each(chunks, lambda i: load_down(0, i).start())
+    for step in range(1, ranks):
+        z_wait(step)
+        x_copy(step).start()
+        c_copy(step).start()
+    for step in range(ranks):
+        place = near.at[rows_of(rank_at(ranks - step)), other_columns]
+        remote(place, place, c_send.at[step], c_recv.at[step], core_peer).wait_recv()
+
+    def product(part, e):
+        lhs = near if part == 0 else far
+        block = weights[pl.ds(part * group + e * ktiles, ktiles)]
+        return jnp.dot(
+            lhs[...], block.reshape(ktiles * TILE, TILE), preferred_element_type=jnp.float32
+        )
+
+    def first_half(e):
+        load_up(0, e).wait()
+        acc[e] = product(0, e)
+
+    early = experts // 2
+    each(early, first_half)
+    for step in range(ranks):
+        x_copy(step).wait_recv()
+        f_copy(step).start()
+    each(experts - early, lambda e: first_half(e + early))
+    each(chunks, lambda i: load_down(1, i).start())
+    for step in range(1, ranks):
+        there = gates.at[rows_of(rank_at(ranks - step)), :]
+        remote(there, there, g_send.at[step - 1], g_recv.at[step - 1], {"expert": rank_at(step)}).wait_recv()
+    for step in range(ranks):
+        place = far.at[rows_of(rank_at(ranks - step)), other_columns]
+        remote(place, place, f_send.at[step], f_recv.at[step], core_peer).wait_recv()
+
+    lane_all = lax.broadcasted_iota(jnp.int32, gates.shape, 1)
+
+    def second_half(e):
+        load_up(1, e).wait()
+        value = acc[e] + product(1, e)
+        share = jnp.sum(jnp.where(lane_all == e, gates[...], 0.0), axis=1, keepdims=True)
+        value = value / (1.0 + jnp.exp(-value)) * share
+        hidden[:, pl.ds(pl.multiple_of(e * TILE, TILE), TILE)] = value.astype(jnp.bfloat16)
+
+    each(experts, second_half)
+
+    def down_chunk(part, i):
+        load_down(part, i).wait()
+        first = 2 * group if part == 0 else 0
+        block = weights[pl.ds(first + i * experts, experts)]
+        value = jnp.dot(
+            hidden[...], block.reshape(experts * TILE, TILE), preferred_element_type=jnp.float32
+        )
+        target = sums_far if part == 0 else sums_near
+        target[:, pl.ds(pl.multiple_of(chunk_at(i) * TILE, TILE), TILE)] = value.astype(jnp.bfloat16)
+
+    front = (chunks + 1) // 2
+    far_pair = remote(sums_far.at[:, other_columns], got_far, p_send.at[0], p_recv.at[0], core_peer)
+    near_pair = remote(sums_near.at[:, other_columns], got_near, p_send.at[1], p_recv.at[1], core_peer)
+    across = remote(pass_far, got_x, p_send.at[2], p_recv.at[2], chip_peer)
+    each(front, lambda i: down_chunk(0, i))
+    far_pair.start()
+    each(chunks - front, lambda i: down_chunk(0, i + front))
+    far_pair.wait_recv()
+    pass_far[...] = (
+        sums_far[:, columns].astype(jnp.float32) + got_far[...].astype(jnp.float32)
+    ).astype(jnp.bfloat16)
+    across.start()
+    each(front, lambda i: down_chunk(1, i))
+    near_pair.start()
+    each(chunks - front, lambda i: down_chunk(1, i + front))
+    near_pair.wait_recv()
+    across.wait_recv()
+    pass_z[...] = (
+        sums_near[:, columns].astype(jnp.float32)
+        + got_near[...].astype(jnp.float32)
+        + got_x[...].astype(jnp.float32)
+    ).astype(jnp.bfloat16)
+
+    def r_copy(step):
+        return remote(
+            pass_z.at[rows_of(rank_at(step)), :], got_z.at[step - 1],
+            r_send.at[step - 1], r_recv.at[step - 1], {"expert": rank_at(step)},
+        )
+
+    for step in range(1, ranks):
+        r_copy(step).start()
+    total = pass_z[rows_of(me), :].astype(jnp.float32)
+    for step in range(1, ranks):
+        r_copy(step).wait_recv()
+        total = total + got_z[step - 1].astype(jnp.float32)
+    out[...] = total.astype(out.dtype)
+    for step in range(1, ranks):
+        z_copy(step).wait_send()
+        g_copy(step).wait_send()
+        r_copy(step).wait_send()
+    for step in range(ranks):
+        c_copy(step).wait_send()
+        x_copy(step).wait_send()
+        f_copy(step).wait_send()
+    far_pair.wait_send()
+    near_pair.wait_send()
+    across.wait_send()
+
+
+def fused(tokens, up_weight, down_weight, expert_ids, route_scores):
+    ranks = lax.axis_size("expert")
+    rows, width = tokens.shape
+    experts, depth, inner = up_weight.shape
+    ktiles = depth // (2 * TILE)
+    every = rows * ranks
+    bf16, f32 = jnp.bfloat16, jnp.float32
+    vmem = pl.BlockSpec(memory_space=pltpu.VMEM)
+    hbm = pl.BlockSpec(memory_space=pl.ANY)
+    dma = pltpu.SemaphoreType.DMA
+    return pl.pallas_call(
+        functools.partial(fused_kernel, ranks),
+        out_shape=jax.ShapeDtypeStruct((rows, width), bf16),
+        in_specs=[vmem, vmem, vmem, hbm, hbm],
+        out_specs=vmem,
+        scratch_shapes=[
+            pltpu.VMEM((3 * experts * ktiles, TILE, TILE), bf16),
+            pltpu.VMEM((every, 2 * width), bf16),
+            pltpu.VMEM((every, 2 * width), bf16),
+            pltpu.VMEM((every, LANES), f32),
+            pltpu.VMEM((ranks - 1, rows, LANES), f32),
+            pltpu.VMEM((experts, every, TILE), f32),
+            pltpu.VMEM((every, experts * TILE), bf16),
+            pltpu.VMEM((every, 2 * width), bf16),
+            pltpu.VMEM((every, 2 * width), bf16),
+            pltpu.VMEM((every, width), bf16),
+            pltpu.VMEM((every, width), bf16),
+            pltpu.VMEM((every, width), bf16),
+            pltpu.VMEM((every, width), bf16),
+            pltpu.VMEM((every, width), bf16),
+            pltpu.VMEM((ranks - 1, rows, width), bf16),
+            dma((2 * experts + 2 * ktiles,)),
+            dma((ranks - 1,)), dma((ranks - 1,)),
+            dma((ranks - 1,)), dma((ranks - 1,)),
+            dma((ranks,)), dma((ranks,)),
+            dma((ranks,)), dma((ranks,)),
+            dma((ranks,)), dma((ranks,)),
+            dma((3,)), dma((3,)),
+            dma((ranks - 1,)), dma((ranks - 1,)),
+        ],
+        compiler_params=pltpu.CompilerParams(
+            collective_id=0, has_side_effects=True, vmem_limit_bytes=60 * 2**20
+        ),
+        cost_estimate=pl.CostEstimate(
+            flops=4 * every * experts * depth * inner,
+            bytes_accessed=4 * experts * depth * inner,
+            transcendentals=every * experts * inner,
+        ),
+    )(
+        tokens, expert_ids, route_scores,
+        up_weight.reshape(experts, depth // TILE, TILE, inner), down_weight,
+    )
+
+
+def local(tokens, up_weight, down_weight, expert_ids, route_scores):
+    ranks, helpers = lax.axis_size("expert"), lax.axis_size("helper")
+    experts, depth, inner = up_weight.shape
+    small = (
+        ranks * tokens.shape[0] <= 128 and helpers == 4 and experts <= 16
+        and depth == 3584 and inner == TILE
+    )
+    run = fused if small else spread
+    return run(tokens, up_weight, down_weight, expert_ids, route_scores)
+
+
 def solution(mesh):
     return jax.shard_map(
         local,

time: 122 us -> 45.9 us (0.38)
  waiting for transfers between devices: 44.6 us -> 0 us
  Pallas kernels: 0 us -> 41.4 us
  matrix products: 25.4 us -> 0 us
  blocking collectives: 23.8 us -> 0 us
  between operations: 13.4 us -> 0.01 us
  starting transfers between devices: 6.36 us -> 0 us
  other arithmetic: 2.21 us -> 0 us
    pallas_call x0 -> x1, Pallas kernels: none -> 41.4 us  [fused(): pl.pallas_call(functools.partial(fused_kernel, ranks), out_shape=jax.Shap...]
    dot_general x1 -> x0, matrix products: 25.4 us -> none  [local(): jnp.einsum('etf,efd->td', hidden, down_weight, preferred_element_type=jnp...]
    unnamed x3 -> x0, waiting for transfers between devices: 24.4 us -> none
    all_gather x2 -> x0, blocking collectives: 23.8 us -> none  [the longest x1 14.5 us: local(): full = lax.all_gather(tokens, 'expert', axis=0, tiled=True)]
    reduce_scatter x1 -> x0, waiting for transfers between devices: 20.1 us -> none  [local(): return lax.psum_scatter(total, 'expert', scatter_dimension=0, tiled=True)]
    all_to_all x1 -> x0, starting transfers between devices: 6.32 us -> none  [local(): lax.all_to_all(table.reshape(-1, expert_ranks, local_count).transpose(1,...]
    unnamed x5 -> x3, local copies, waits for them, and re-layouts: 4.57 us -> 4.17 us
  transfers between devices with their start and end apart: 3 -> 0, of which waited for: 2 -> 0; matrix products, arithmetic and copies ran while one was open for 0% -> 0% of each run, Pallas kernels for 0% -> 0%
where the time goes in v2:
time: 45.9 us; the launch traced here: 45.6 us
  Pallas kernels  41.4 us (90%)
  local copies, waits for them, and re-layouts  4.17 us (9%)
    pallas_call x1, Pallas kernels, fused(): pl.pallas_call(functools.partial(fused_kernel, ranks), out_shape=jax.Shap...  41.4 us
    unnamed x3, local copies, waits for them, and re-layouts  4.17 us

profile of v2, /device:TPU:0, one launch (start us, length us, event | category | flops | bytes accessed | tf_op | source)
XLA Modules:
  0.0 45.6 jit_solution(6569141944991086354)
XLA Ops:
  0.0 1.4 %copy.6.ids = s32[32,8]{1,0:T(8,128)} copy(s32[32,8]{0,1:T(8,128)} %param.8) | data formatting | bytes 2048 | tf_op args[3]
  1.4 1.4 %copy.7.scores = f32[32,8]{1,0:T(8,128)} copy(f32[32,8]{0,1:T(8,128)} %param.9) | data formatting | bytes 2048 | tf_op args[4]
  2.7 41.4 %shard_map.55 = bf16[32,896]{1,0:T(8,128)(2,1)} custom-call(bf16[32,896]{1,0:T(8,128)(2,1)} %tokens.1, s32[32,8]{1,0:T(8,128)} %copy.6.ids, f32[32,8]{1,0:T(8,128)} %copy.7.scores, bf16[16,14,256,256]{3,2,1,0:T(8,128)(2,1)} %bitcast.1, bf16[16,256,3584]{2,1,0:T(8,128)(2,1)} %down.1), custom_call_target="tpu_custom_call" | custom-call | flops 7516192768 | bytes 58720256 | tf_op jit(solution)/shard_map/pallas_call | solution.py:262
  44.1 1.4 %copy.9 = bf16[32,896]{1,0:T(8,128)(2,1)} copy(bf16[32,896]{1,0:T(8,128)(2,1)} %shard_map.55) | data formatting | bytes 114688

commit v3 on v2

--- a/solution.py
+++ b/solution.py
@@ -9,6 +9,11 @@
 
 TILE = 256
 LANES = 128
+PIECES = (
+    (0, 0, 256), (0, 256, 256), (1, 0, 256), (1, 256, 256),
+    (0, 512, 256), (0, 768, 128), (1, 512, 256), (1, 768, 128),
+)
+SUBS = ((0, 512), (512, 384))
 MESH = pl.DeviceIdType.MESH
 
 
@@ -43,7 +48,6 @@
 ):
     rows, width = tokens.shape
     experts, ktiles = up.shape[0], up.shape[1] // 2
-    chunks = ktiles
     group = experts * ktiles
     me = lax.axis_index("expert")
     helper = lax.axis_index("helper")
@@ -67,18 +71,24 @@
             weight_sem.at[part * experts + e],
         )
 
-    def chunk_at(i):
-        return jnp.where(core == 1, i, chunks - 1 - i)
+    def piece_at(part, i):
+        half = 1 - chip if part == 0 else chip
+        owner = 1 - core if PIECES[i][0] == 0 else core
+        return owner * width + PIECES[i][1], (half * 2 + owner) * width + PIECES[i][1]
 
     def load_down(part, i):
-        half = 1 - chip if part == 0 else chip
-        first = 2 * group if part == 0 else 0
-        column = pl.multiple_of((half * chunks + chunk_at(i)) * TILE, TILE)
+        span = PIECES[i][2]
+        column = pl.multiple_of(piece_at(part, i)[1], LANES)
         return pltpu.make_async_copy(
-            down.at[:, :, pl.ds(column, TILE)],
-            weights.at[pl.ds(first + i * experts, experts)],
-            weight_sem.at[2 * experts + part * chunks + i],
-        )
+            down.at[:, :, pl.ds(column, span)],
+            weights.at[pl.ds(first_tile(part, i), experts), :, pl.ds(0, span)],
+            weight_sem.at[2 * experts + part * len(PIECES) + i],
+        )
+
+    def first_tile(part, i):
+        if part == 0:
+            return 2 * group + i * experts
+        return i * experts if (i + 1) * experts <= group else 2 * group + len(PIECES) * experts
 
     def remote(src, dst, send, recv, device):
         return pltpu.make_async_remote_copy(
@@ -96,9 +106,9 @@
     pl.semaphore_signal(barrier, inc=1, device_id=chip_peer, device_id_type=MESH)
     each(experts, lambda e: load_up(0, e).start())
     near[rows_of(me), columns] = tokens[...]
-    score = scores[...]
+    score = scores[...].T
     gate = 2.5 * score / jnp.sum(score, axis=1, keepdims=True)
-    named = ids[...]
+    named = ids[...].T
     lane = lax.broadcasted_iota(jnp.int32, (rows, LANES), 1)
     for step in range(ranks):
         base = rank_at(step) * experts
@@ -145,7 +155,8 @@
     for step in range(1, ranks):
         g_copy(step).start()
     each(experts, lambda e: load_up(1, e).start())
-    each(chunks, lambda i: load_down(0, i).start())
+    for i in range(len(PIECES)):
+        load_down(0, i).start()
     for step in range(1, ranks):
         z_wait(step)
         x_copy(step).start()
@@ -171,7 +182,8 @@
         x_copy(step).wait_recv()
         f_copy(step).start()
     each(experts - early, lambda e: first_half(e + early))
-    each(chunks, lambda i: load_down(1, i).start())
+    for i in range(len(PIECES)):
+        load_down(1, i).start()
     for step in range(1, ranks):
         there = gates.at[rows_of(rank_at(ranks - step)), :]
         remote(there, there, g_send.at[step - 1], g_recv.at[step - 1], {"expert": rank_at(step)}).wait_recv()
@@ -190,63 +202,87 @@
 
     each(experts, second_half)
 
-    def down_chunk(part, i):
+    def down_piece(part, i):
         load_down(part, i).wait()
-        first = 2 * group if part == 0 else 0
-        block = weights[pl.ds(first + i * experts, experts)]
+        span = PIECES[i][2]
+        block = weights[pl.ds(first_tile(part, i), experts), :, pl.ds(0, span)]
         value = jnp.dot(
-            hidden[...], block.reshape(experts * TILE, TILE), preferred_element_type=jnp.float32
+            hidden[...], block.reshape(experts * TILE, span), preferred_element_type=jnp.float32
         )
         target = sums_far if part == 0 else sums_near
-        target[:, pl.ds(pl.multiple_of(chunk_at(i) * TILE, TILE), TILE)] = value.astype(jnp.bfloat16)
-
-    front = (chunks + 1) // 2
-    far_pair = remote(sums_far.at[:, other_columns], got_far, p_send.at[0], p_recv.at[0], core_peer)
-    near_pair = remote(sums_near.at[:, other_columns], got_near, p_send.at[1], p_recv.at[1], core_peer)
-    across = remote(pass_far, got_x, p_send.at[2], p_recv.at[2], chip_peer)
-    each(front, lambda i: down_chunk(0, i))
-    far_pair.start()
-    each(chunks - front, lambda i: down_chunk(0, i + front))
-    far_pair.wait_recv()
-    pass_far[...] = (
-        sums_far[:, columns].astype(jnp.float32) + got_far[...].astype(jnp.float32)
-    ).astype(jnp.bfloat16)
-    across.start()
-    each(front, lambda i: down_chunk(1, i))
-    near_pair.start()
-    each(chunks - front, lambda i: down_chunk(1, i + front))
-    near_pair.wait_recv()
-    across.wait_recv()
-    pass_z[...] = (
-        sums_near[:, columns].astype(jnp.float32)
-        + got_near[...].astype(jnp.float32)
-        + got_x[...].astype(jnp.float32)
-    ).astype(jnp.bfloat16)
-
-    def r_copy(step):
+        place = pl.multiple_of(piece_at(part, i)[0], LANES)
+        target[:, pl.ds(place, span)] = value.astype(jnp.bfloat16)
+
+    def block_of(owner, sub):
+        first, span = SUBS[sub]
+        return pl.ds(pl.multiple_of(owner * width + first, LANES), span)
+
+    def sub_of(sub):
+        return pl.ds(SUBS[sub][0], SUBS[sub][1])
+
+    def pair_copy(part, sub):
+        source, sink = (sums_far, got_far) if part == 0 else (sums_near, got_near)
+        k = part * 2 + sub
         return remote(
-            pass_z.at[rows_of(rank_at(step)), :], got_z.at[step - 1],
-            r_send.at[step - 1], r_recv.at[step - 1], {"expert": rank_at(step)},
-        )
-
-    for step in range(1, ranks):
-        r_copy(step).start()
-    total = pass_z[rows_of(me), :].astype(jnp.float32)
-    for step in range(1, ranks):
-        r_copy(step).wait_recv()
-        total = total + got_z[step - 1].astype(jnp.float32)
-    out[...] = total.astype(out.dtype)
+            source.at[:, block_of(1 - core, sub)], sink.at[:, sub_of(sub)],
+            p_send.at[k], p_recv.at[k], core_peer,
+        )
+
+    def across(sub):
+        return remote(
+            pass_far.at[:, sub_of(sub)], got_x.at[:, sub_of(sub)],
+            p_send.at[4 + sub], p_recv.at[4 + sub], chip_peer,
+        )
+
+    def r_copy(step, sub):
+        k = (step - 1) * 2 + sub
+        return remote(
+            pass_z.at[rows_of(rank_at(step)), sub_of(sub)], got_z.at[step - 1, :, sub_of(sub)],
+            r_send.at[k], r_recv.at[k], {"expert": rank_at(step)},
+        )
+
+    for part in range(2):
+        for sub in range(2):
+            down_piece(part, 4 * sub)
+            down_piece(part, 4 * sub + 1)
+            pair_copy(part, sub).start()
+            down_piece(part, 4 * sub + 2)
+            down_piece(part, 4 * sub + 3)
+            pair_copy(part, sub).wait_recv()
+            if part == 0:
+                pass_far[:, sub_of(sub)] = (
+                    sums_far[:, block_of(core, sub)].astype(jnp.float32)
+                    + got_far[:, sub_of(sub)].astype(jnp.float32)
+                ).astype(jnp.bfloat16)
+                across(sub).start()
+            else:
+                across(sub).wait_recv()
+                pass_z[:, sub_of(sub)] = (
+                    sums_near[:, block_of(core, sub)].astype(jnp.float32)
+                    + got_near[:, sub_of(sub)].astype(jnp.float32)
+                    + got_x[:, sub_of(sub)].astype(jnp.float32)
+                ).astype(jnp.bfloat16)
+                for step in range(1, ranks):
+                    r_copy(step, sub).start()
+    for sub in range(2):
+        total = pass_z[rows_of(me), sub_of(sub)].astype(jnp.float32)
+        for step in range(1, ranks):
+            r_copy(step, sub).wait_recv()
+            total = total + got_z[step - 1, :, sub_of(sub)].astype(jnp.float32)
+        out[:, sub_of(sub)] = total.astype(out.dtype)
     for step in range(1, ranks):
         z_copy(step).wait_send()
         g_copy(step).wait_send()
-        r_copy(step).wait_send()
+        r_copy(step, 0).wait_send()
+        r_copy(step, 1).wait_send()
     for step in range(ranks):
         c_copy(step).wait_send()
         x_copy(step).wait_send()
         f_copy(step).wait_send()
-    far_pair.wait_send()
-    near_pair.wait_send()
-    across.wait_send()
+    for sub in range(2):
+        pair_copy(0, sub).wait_send()
+        pair_copy(1, sub).wait_send()
+        across(sub).wait_send()
 
 
 def fused(tokens, up_weight, down_weight, expert_ids, route_scores):
@@ -265,7 +301,7 @@
         in_specs=[vmem, vmem, vmem, hbm, hbm],
         out_specs=vmem,
         scratch_shapes=[
-            pltpu.VMEM((3 * experts * ktiles, TILE, TILE), bf16),
+            pltpu.VMEM((experts * (2 * ktiles + len(PIECES) + 1), TILE, TILE), bf16),
             pltpu.VMEM((every, 2 * width), bf16),
             pltpu.VMEM((every, 2 * width), bf16),
             pltpu.VMEM((every, LANES), f32),
@@ -280,14 +316,14 @@
             pltpu.VMEM((every, width), bf16),
             pltpu.VMEM((every, width), bf16),
             pltpu.VMEM((ranks - 1, rows, width), bf16),
-            dma((2 * experts + 2 * ktiles,)),
+            dma((2 * experts + 2 * len(PIECES),)),
             dma((ranks - 1,)), dma((ranks - 1,)),
             dma((ranks - 1,)), dma((ranks - 1,)),
             dma((ranks,)), dma((ranks,)),
             dma((ranks,)), dma((ranks,)),
             dma((ranks,)), dma((ranks,)),
-            dma((3,)), dma((3,)),
-            dma((ranks - 1,)), dma((ranks - 1,)),
+            dma((6,)), dma((6,)),
+            dma((2 * (ranks - 1),)), dma((2 * (ranks - 1),)),
         ],
         compiler_params=pltpu.CompilerParams(
             collective_id=0, has_side_effects=True, vmem_limit_bytes=60 * 2**20
@@ -298,7 +334,7 @@
             transcendentals=every * experts * inner,
         ),
     )(
-        tokens, expert_ids, route_scores,
+        tokens, expert_ids.T, route_scores.T,
         up_weight.reshape(experts, depth // TILE, TILE, inner), down_weight,
     )
 
@@ -307,8 +343,8 @@
     ranks, helpers = lax.axis_size("expert"), lax.axis_size("helper")
     experts, depth, inner = up_weight.shape
     small = (
-        ranks * tokens.shape[0] <= 128 and helpers == 4 and experts <= 16
-        and depth == 3584 and inner == TILE
+        ranks * tokens.shape[0] <= 128 and helpers == 4 and experts == 16
+        and tokens.shape[1] == 896 and inner == TILE
     )
     run = fused if small else spread
     return run(tokens, up_weight, down_weight, expert_ids, route_scores)

time: 45.9 us -> 43.4 us (0.946)
  local copies, waits for them, and re-layouts: 4.17 us -> 1.45 us
    unnamed x3 -> x1, local copies, waits for them, and re-layouts: 4.17 us -> 1.45 us
where the time goes in v3:
time: 43.4 us; the launch traced here: 43.2 us
  Pallas kernels  41.8 us (96%)
  local copies, waits for them, and re-layouts  1.45 us (3%)
    pallas_call x1, Pallas kernels, fused(): pl.pallas_call(functools.partial(fused_kernel, ranks), out_shape=jax.Shap...  41.8 us
    unnamed x1, local copies, waits for them, and re-layouts  1.45 us

profile of v3, /device:TPU:0, one launch (start us, length us, event | category | flops | bytes accessed | tf_op | source)
XLA Modules:
  0.0 43.2 jit_solution(15420203563960057276)
XLA Ops:
  0.0 41.8 %shard_map.55 = bf16[32,896]{1,0:T(8,128)(2,1)} custom-call(bf16[32,896]{1,0:T(8,128)(2,1)} %tokens.1, s32[8,32]{1,0:T(8,128)} %bitcast.4, f32[8,32]{1,0:T(8,128)} %bitcast.5, bf16[16,14,256,256]{3,2,1,0:T(8,128)(2,1)} %bitcast.3, bf16[16,256,3584]{2,1,0:T(8,128)(2,1)} %down.1), custom_call_target="tpu_custom_call" | custom-call | flops 7516192768 | bytes 58720256 | tf_op jit(solution)/shard_map/pallas_call | solution.py:298
  41.8 1.4 %copy.7 = bf16[32,896]{1,0:T(8,128)(2,1)} copy(bf16[32,896]{1,0:T(8,128)(2,1)} %shard_map.55) | data formatting | bytes 114688
